TPU v7x, 128 devices: a whole 4x4x4 slice. The times are simulated.
128 devices in a mesh: dp: 8 (over y_lo, x), ctx: 16 (over z, y_hi, core).
Axes of the slice: x: 4, y: 4 (y_hi: 2, y_lo: 2; y = y_hi * 2 + y_lo), z: 4, core: 2. Of those that a mesh axis runs over, the one named last changes fastest.
Arguments:
- query_one: bfloat16 [16384, 4096], P(('dp', 'ctx')), parts along dimension 0, may hold values from -64 to 64
- query_two: bfloat16 [16384, 4096], P(('dp', 'ctx')), parts along dimension 0, may hold values from -64 to 64
- shared_keys: bfloat16 [16384, 512], P(('dp', 'ctx')), parts along dimension 0, may hold values from -8 to 8
- common_values: bfloat16 [16384, 512], P(('dp', 'ctx')), parts along dimension 0, may hold values from -6 to 6
- cotangent_one: bfloat16 [16384, 4096], P(('dp', 'ctx')), parts along dimension 0, may hold values from -96 to 96
- cotangent_two: bfloat16 [16384, 4096], P(('dp', 'ctx')), parts along dimension 0, may hold values from -96 to 96
- span_order: int32 [256], P('dp'), parts along dimension 0, may hold values from 0 to 31, each once
- lengths: int32 [64], P('dp'), parts along dimension 0, may hold values from 1 to 1024, 2048 in all
Outputs:
- query_grad_one: bfloat16 [16384, 4096], P(('dp', 'ctx')), parts along dimension 0
- query_grad_two: bfloat16 [16384, 4096], P(('dp', 'ctx')), parts along dimension 0
- key_grad: bfloat16 [16384, 512], P(('dp', 'ctx')), parts along dimension 0
- value_grad: bfloat16 [16384, 512], P(('dp', 'ctx')), parts along dimension 0
There are 8 independent parts, one for each index of `dp`. A program takes and returns all parts, laid end to end along the dimension named above; each array names one. Nothing has to cross between parts.
Inputs may be any that keep to these rules, and one draw needn't show every extreme that they name: `span_order`: a permutation. `lengths`: they sum to 2048; the largest is exactly 1024.
All inputs are finite; a program needn't handle non-finite values.
Results may differ from a plain program's by a relative error of at most 0.0075.
Values may be sent and summed in bfloat16 or wider, within the bound.
No kernel may reach another device: no remote copies, remote signals or barrier semaphores. Data moves between devices by JAX's collectives and lax.ppermute only.
A program may use at most 320 MiB of HBM per device.

v0:
```python
import jax
import jax.numpy as jnp
from jax import lax
from jax.sharding import PartitionSpec as P

HEAD_SIZE = 128
KEY_VALUE_HEADS = 4
QUERY_PER_KEY = 8
HALF = 64


def head_group(group_width, queries, key_rows, values, cotangent, visible):
    scale = HEAD_SIZE ** (-0.5)
    rows_here = queries.shape[0]
    query_block = queries[
        :, group_width * QUERY_PER_KEY * HEAD_SIZE : (group_width + 1) * QUERY_PER_KEY * HEAD_SIZE
    ].reshape(rows_here, QUERY_PER_KEY, HEAD_SIZE)
    cot_block = cotangent[
        :, group_width * QUERY_PER_KEY * HEAD_SIZE : (group_width + 1) * QUERY_PER_KEY * HEAD_SIZE
    ].reshape(rows_here, QUERY_PER_KEY, HEAD_SIZE)
    key_block = key_rows[:, group_width * HEAD_SIZE : (group_width + 1) * HEAD_SIZE]
    value_block = values[:, group_width * HEAD_SIZE : (group_width + 1) * HEAD_SIZE]
    scores = (
        jnp.einsum("thd,kd->htk", query_block, key_block, preferred_element_type=jnp.float32)
        * scale
    )
    scores = jnp.where(visible[None], scores, -1e30)
    peak = jnp.max(scores, axis=-1, keepdims=True)
    expo = jnp.exp(scores - peak)
    probs = expo / jnp.sum(expo, axis=-1, keepdims=True)
    probs_low = probs.astype(jnp.bfloat16)
    dprobs = jnp.einsum("thd,kd->htk", cot_block, value_block, preferred_element_type=jnp.float32)
    dsum = jnp.sum(probs * dprobs, axis=-1, keepdims=True)
    dscores_low = (probs * (dprobs - dsum) * scale).astype(jnp.bfloat16)
    query_part = jnp.einsum(
        "htk,kd->thd", dscores_low, key_block, preferred_element_type=jnp.float32
    ).reshape(rows_here, QUERY_PER_KEY * HEAD_SIZE)
    key_part = jnp.einsum(
        "htk,thd->kd", dscores_low, query_block, preferred_element_type=jnp.float32
    )
    value_part = jnp.einsum("htk,thd->kd", probs_low, cot_block, preferred_element_type=jnp.float32)
    return (query_part, key_part, value_part)


def layer_grads(queries, key_rows, values, cotangent, visible):
    query_parts, key_parts, value_parts = ([], [], [])
    for group_width in range(KEY_VALUE_HEADS):
        query_part, key_part, value_part = head_group(
            group_width, queries, key_rows, values, cotangent, visible
        )
        query_parts.append(query_part)
        key_parts.append(key_part)
        value_parts.append(value_part)
    return (
        jnp.concatenate(query_parts, axis=1),
        jnp.concatenate(key_parts, axis=1),
        jnp.concatenate(value_parts, axis=1),
    )


def local(
    query_one,
    query_two,
    shared_keys,
    common_values,
    cotangent_one,
    cotangent_two,
    span_order,
    lengths,
):
    all_keys, all_values = (
        lax.all_gather(shared_keys, "ctx", axis=0, tiled=True),
        lax.all_gather(common_values, "ctx", axis=0, tiled=True),
    )
    rows_here = query_one.shape[0]
    total_rows = all_keys.shape[0]
    device_index = lax.axis_index("ctx")
    rows = jnp.arange(total_rows, dtype=jnp.int32)
    slots = jnp.arange(span_order.shape[0], dtype=jnp.int32)
    one_hot = ((rows // HALF)[:, None] == slots[None, :]).astype(jnp.int32)
    positions = jnp.sum(one_hot * span_order[None, :], axis=1) * HALF + rows % HALF
    ends = jnp.cumsum(lengths)
    documents = jnp.sum((positions[:, None] >= ends[None, :]).astype(jnp.int32), axis=1)
    start_row = device_index * rows_here
    local_pos = lax.dynamic_slice_in_dim(positions, start_row, rows_here)
    local_doc = lax.dynamic_slice_in_dim(documents, start_row, rows_here)
    visible = (positions[None, :] <= local_pos[:, None]) & (
        documents[None, :] == local_doc[:, None]
    )
    grad_q1, grad_k1, grad_v1 = layer_grads(query_one, all_keys, all_values, cotangent_one, visible)
    grad_q2, grad_k2, grad_v2 = layer_grads(query_two, all_keys, all_values, cotangent_two, visible)
    width = grad_k1.shape[1]
    stacked = jnp.concatenate([grad_k1 + grad_k2, grad_v1 + grad_v2], axis=1)
    summed = lax.psum_scatter(stacked, "ctx", scatter_dimension=0, tiled=True)
    key_sum = summed[:, :width]
    value_sum = summed[:, width:]
    return (
        grad_q1.astype(jnp.bfloat16),
        grad_q2.astype(jnp.bfloat16),
        key_sum.astype(jnp.bfloat16),
        value_sum.astype(jnp.bfloat16),
    )


def solution(mesh):
    in_specs = (
        P(("dp", "ctx"), None),
        P(("dp", "ctx"), None),
        P(("dp", "ctx"), None),
        P(("dp", "ctx"), None),
        P(("dp", "ctx"), None),
        P(("dp", "ctx"), None),
        P("dp"),
        P("dp"),
    )
    out_specs = (
        P(("dp", "ctx"), None),
        P(("dp", "ctx"), None),
        P(("dp", "ctx"), None),
        P(("dp", "ctx"), None),
    )
    return jax.shard_map(local, mesh=mesh, in_specs=in_specs, out_specs=out_specs, check_vma=False)
```

profile of v0, /device:TPU:1, one launch (start us, length us, event | category | flops | bytes accessed | tf_op | source)
XLA Modules:
  0.0 492.2 jit_solution(15425951806183071014)
XLA Ops:
  24.2 37.6 %all-gather.3.cloned.1.call-done = bf16[2048,512]{1,0:T(8,128)(2,1)} async-done(((bf16[128,512]{1,0:T(8,128)(2,1)}), bf16[2048,512]{1,0:T(8,128)(2,1)}) %all-gather.3.cloned.1.call-update) | async-done | bytes 2097168 | tf_op jit(solution)/shard_map/all_gather | solution.py:72
  61.8 7.1 %fusion.241 = (f32[8,128]{1,0:T(8,128)S(1)}, f32[8,128,2048]{1,2,0:T(8,128)}) fusion(pred[128,2048]{0,1:T(8,128)(4,1)S(1)} %compare_and_fusion, bf16[128,8,128]{0,2,1:T(8,128)(2,1)} %bitcast.560, bf16[2048,512]{1,0:T(8,128)(2,1)} %all-gather.3.cloned.1.call-done), kind=kOutput, calls=%fused_computation.278 | convolution fusion | flops 545261568 | bytes 9441280 | tf_op jit(solution)/shard_map/sub | solution.py:29
  68.9 5.9 %fusion.141 = f32[2048,128]{0,1:T(8,128)} fusion(bf16[128,8,128]{0,2,1:T(8,128)(2,1)S(1)} %bitcast.544, f32[8,128,2048]{1,2,0:T(8,128)} %get-tuple-element.43, f32[8,128]{1,0:T(8,128)S(1)} %get-tuple-element.42), kind=kOutput, calls=%fused_computation.170 | convolution fusion | flops 541065216 | bytes 9703424 | tf_op jit(solution)/shard_map/htk,thd->kd/dot_general | solution.py:41
  74.8 35.8 %all-gather.5.cloned.1.call-done = bf16[2048,512]{1,0:T(8,128)(2,1)} async-done(((bf16[128,512]{1,0:T(8,128)(2,1)}), bf16[2048,512]{1,0:T(8,128)(2,1)}) %all-gather.5.cloned.1.call-update) | async-done | bytes 2097168 | tf_op jit(solution)/shard_map/all_gather | solution.py:73
  116.1 14.5 %fusion.112 = f32[2048,128]{0,1:T(8,128)} fusion(bf16[128,8,128]{0,2,1:T(8,128)(2,1)S(1)} %bitcast.561, f32[2048,128,8]{1,0,2:T(8,128)} %fusion.174, f32[8,128,2048]{1,2,0:T(8,128)} %get-tuple-element.43, f32[8,128]{1,0:T(8,128)S(1)} %get-tuple-element.42), kind=kOutput, calls=%fused_computation.155 | convolution fusion | flops 551554048 | bytes 18092032 | tf_op jit(solution)/shard_map/htk,thd->kd/dot_general | solution.py:38
  130.6 7.0 %fusion.243 = (f32[8,128]{1,0:T(8,128)S(1)}, f32[8,128,2048]{1,2,0:T(8,128)}) fusion(pred[128,2048]{0,1:T(8,128)(4,1)S(1)} %compare_and_fusion, bf16[128,8,128]{0,2,1:T(8,128)(2,1)S(1)} %bitcast.559, bf16[2048,512]{1,0:T(8,128)(2,1)} %all-gather.3.cloned.1.call-done), kind=kOutput, calls=%fused_computation.280 | convolution fusion | flops 545261568 | bytes 9441280 | tf_op jit(solution)/shard_map/sub | solution.py:29
  137.7 6.0 %fusion.135 = f32[2048,128]{0,1:T(8,128)} fusion(bf16[128,8,128]{0,2,1:T(8,128)(2,1)S(1)} %bitcast.542, f32[8,128,2048]{1,2,0:T(8,128)} %get-tuple-element.47, f32[8,128]{1,0:T(8,128)S(1)} %get-tuple-element.46), kind=kOutput, calls=%fused_computation.168 | convolution fusion | flops 541065216 | bytes 9703424 | tf_op jit(solution)/shard_map/htk,thd->kd/dot_general | solution.py:41
  148.1 14.2 %fusion.114 = f32[2048,128]{0,1:T(8,128)} fusion(bf16[128,8,128]{0,2,1:T(8,128)(2,1)} %bitcast.558, f32[2048,128,8]{1,0,2:T(8,128)} %fusion.170, f32[8,128,2048]{1,2,0:T(8,128)} %get-tuple-element.47, f32[8,128]{1,0:T(8,128)S(1)} %get-tuple-element.46), kind=kOutput, calls=%fused_computation.157 | convolution fusion | flops 551554048 | bytes 18092032 | tf_op jit(solution)/shard_map/htk,thd->kd/dot_general | solution.py:38
  162.3 7.1 %fusion.242 = (f32[8,128]{1,0:T(8,128)S(1)}, f32[8,128,2048]{1,2,0:T(8,128)}) fusion(pred[128,2048]{0,1:T(8,128)(4,1)S(1)} %copy-done.13, bf16[128,8,128]{0,2,1:T(8,128)(2,1)} %bitcast.556, bf16[2048,512]{1,0:T(8,128)(2,1)} %all-gather.3.cloned.1.call-done), kind=kOutput, calls=%fused_computation.279 | convolution fusion | flops 545261568 | bytes 9441280 | tf_op jit(solution)/shard_map/sub | solution.py:29
  179.9 14.2 %fusion.113 = f32[2048,128]{0,1:T(8,128)} fusion(bf16[128,8,128]{0,2,1:T(8,128)(2,1)} %bitcast.557, f32[2048,128,8]{1,0,2:T(8,128)} %fusion.172, f32[8,128,2048]{1,2,0:T(8,128)} %get-tuple-element.45, f32[8,128]{1,0:T(8,128)S(1)} %get-tuple-element.44), kind=kOutput, calls=%fused_computation.156 | convolution fusion | flops 551554048 | bytes 18092032 | tf_op jit(solution)/shard_map/htk,thd->kd/dot_general | solution.py:38
  194.1 7.0 %fusion.244 = (f32[8,128]{1,0:T(8,128)S(1)}, f32[8,128,2048]{1,2,0:T(8,128)}) fusion(pred[128,2048]{0,1:T(8,128)(4,1)S(1)} %copy-done.13, bf16[128,8,128]{0,2,1:T(8,128)(2,1)S(1)} %bitcast.554, bf16[2048,512]{1,0:T(8,128)(2,1)} %all-gather.3.cloned.1.call-done), kind=kOutput, calls=%fused_computation.281 | convolution fusion | flops 545261568 | bytes 9441280 | tf_op jit(solution)/shard_map/sub | solution.py:29
  201.1 5.9 %fusion.132 = f32[2048,128]{0,1:T(8,128)} fusion(bf16[128,8,128]{0,2,1:T(8,128)(2,1)S(1)} %bitcast.538, f32[8,128,2048]{1,2,0:T(8,128)} %get-tuple-element.49, f32[8,128]{1,0:T(8,128)S(1)} %get-tuple-element.48), kind=kOutput, calls=%fused_computation.167 | convolution fusion | flops 541065216 | bytes 9703424 | tf_op jit(solution)/shard_map/htk,thd->kd/dot_general | solution.py:41
  211.5 14.8 %fusion.115 = f32[2048,128]{0,1:T(8,128)} fusion(bf16[128,8,128]{0,2,1:T(8,128)(2,1)S(1)} %bitcast.555, f32[2048,128,8]{1,0,2:T(8,128)} %fusion.168, f32[8,128,2048]{1,2,0:T(8,128)} %get-tuple-element.49, f32[8,128]{1,0:T(8,128)S(1)} %get-tuple-element.48), kind=kOutput, calls=%fused_computation.158 | convolution fusion | flops 551554048 | bytes 18092032 | tf_op jit(solution)/shard_map/htk,thd->kd/dot_general | solution.py:38
  226.3 7.0 %fusion.237 = (f32[8,128]{1,0:T(8,128)S(1)}, f32[8,128,2048]{1,2,0:T(8,128)}) fusion(pred[128,2048]{0,1:T(8,128)(4,1)S(1)} %copy-done.13, bf16[128,8,128]{0,2,1:T(8,128)(2,1)S(1)} %bitcast.552, bf16[2048,512]{1,0:T(8,128)(2,1)} %all-gather.3.cloned.1.call-done), kind=kOutput, calls=%fused_computation.274 | convolution fusion | flops 545261568 | bytes 9441280 | tf_op jit(solution)/shard_map/sub | solution.py:29
  243.6 14.4 %fusion.116 = f32[2048,128]{0,1:T(8,128)} fusion(bf16[128,8,128]{0,2,1:T(8,128)(2,1)S(1)} %bitcast.553, f32[2048,128,8]{1,0,2:T(8,128)} %fusion.175, f32[8,128,2048]{1,2,0:T(8,128)} %get-tuple-element.35, f32[8,128]{1,0:T(8,128)S(1)} %get-tuple-element.34), kind=kOutput, calls=%fused_computation.159 | convolution fusion | flops 551554048 | bytes 18092032 | tf_op jit(solution)/shard_map/htk,thd->kd/dot_general | solution.py:38
  258.0 7.0 %fusion.239 = (f32[8,128]{1,0:T(8,128)S(1)}, f32[8,128,2048]{1,2,0:T(8,128)}) fusion(pred[128,2048]{0,1:T(8,128)(4,1)S(1)} %copy-done.13, bf16[128,8,128]{0,2,1:T(8,128)(2,1)S(1)} %bitcast.550, bf16[2048,512]{1,0:T(8,128)(2,1)} %all-gather.3.cloned.1.call-done), kind=kOutput, calls=%fused_computation.276 | convolution fusion | flops 545261568 | bytes 9441280 | tf_op jit(solution)/shard_map/sub | solution.py:29
  275.5 14.6 %fusion.118 = f32[2048,128]{0,1:T(8,128)} fusion(bf16[128,8,128]{0,2,1:T(8,128)(2,1)S(1)} %bitcast.551, f32[2048,128,8]{1,0,2:T(8,128)} %fusion.171, f32[8,128,2048]{1,2,0:T(8,128)} %get-tuple-element.39, f32[8,128]{1,0:T(8,128)S(1)} %get-tuple-element.38), kind=kOutput, calls=%fused_computation.161 | convolution fusion | flops 551554048 | bytes 18092032 | tf_op jit(solution)/shard_map/htk,thd->kd/dot_general | solution.py:38
  290.0 7.1 %fusion.238 = (f32[8,128]{1,0:T(8,128)S(1)}, f32[8,128,2048]{1,2,0:T(8,128)}) fusion(pred[128,2048]{0,1:T(8,128)(4,1)S(1)} %copy-done.13, bf16[128,8,128]{0,2,1:T(8,128)(2,1)S(1)} %bitcast.548, bf16[2048,512]{1,0:T(8,128)(2,1)} %all-gather.3.cloned.1.call-done), kind=kOutput, calls=%fused_computation.275 | convolution fusion | flops 545261568 | bytes 9441280 | tf_op jit(solution)/shard_map/sub | solution.py:29
  297.2 5.9 %fusion.126 = f32[2048,128]{0,1:T(8,128)} fusion(bf16[128,8,128]{0,2,1:T(8,128)(2,1)S(1)} %bitcast.532, f32[8,128,2048]{1,2,0:T(8,128)} %get-tuple-element.37, f32[8,128]{1,0:T(8,128)S(1)} %get-tuple-element.36), kind=kOutput, calls=%fused_computation.165 | convolution fusion | flops 541065216 | bytes 9703424 | tf_op jit(solution)/shard_map/htk,thd->kd/dot_general | solution.py:41
  307.5 14.3 %fusion.117 = f32[2048,128]{0,1:T(8,128)} fusion(bf16[128,8,128]{0,2,1:T(8,128)(2,1)S(1)} %bitcast.549, f32[2048,128,8]{1,0,2:T(8,128)} %fusion.173, f32[8,128,2048]{1,2,0:T(8,128)} %get-tuple-element.37, f32[8,128]{1,0:T(8,128)S(1)} %get-tuple-element.36), kind=kOutput, calls=%fused_computation.160 | convolution fusion | flops 551554048 | bytes 18092032 | tf_op jit(solution)/shard_map/htk,thd->kd/dot_general | solution.py:38
  321.9 7.1 %fusion.240 = (f32[8,128]{1,0:T(8,128)S(1)}, f32[8,128,2048]{1,2,0:T(8,128)}) fusion(pred[128,2048]{0,1:T(8,128)(4,1)S(1)} %copy-done.14, bf16[128,8,128]{0,2,1:T(8,128)(2,1)S(1)} %bitcast.546, bf16[2048,512]{1,0:T(8,128)(2,1)} %all-gather.3.cloned.1.call-done), kind=kOutput, calls=%fused_computation.277 | convolution fusion | flops 545261568 | bytes 9441280 | tf_op jit(solution)/shard_map/sub | solution.py:29
  339.3 14.4 %fusion.119 = f32[2048,128]{0,1:T(8,128)} fusion(bf16[128,8,128]{0,2,1:T(8,128)(2,1)S(1)} %bitcast.547, f32[2048,128,8]{1,0,2:T(8,128)} %fusion.169, f32[8,128,2048]{1,2,0:T(8,128)} %get-tuple-element.41, f32[8,128]{1,0:T(8,128)S(1)} %get-tuple-element.40), kind=kOutput, calls=%fused_computation.162 | convolution fusion | flops 551554048 | bytes 18092032 | tf_op jit(solution)/shard_map/htk,thd->kd/dot_general | solution.py:38
  353.7 8.1 %maximum_add_fusion = (f32[2048,512]{0,1:T(8,128)S(1)}, f32[2048,512]{0,1:T(8,128)}) fusion(f32[2048,128]{0,1:T(8,128)} %fusion.116, f32[2048,128]{0,1:T(8,128)} %fusion.117, f32[2048,128]{0,1:T(8,128)} %fusion.118, f32[2048,128]{0,1:T(8,128)} %fusion.119, f32[2048,128]{0,1:T(8,128)S(1)} %copy-done.5, f32[2048,128]{0,1:T(8,128)} %fusion.113, ...), kind=kLoop, calls=%fused_computation.81 | loop fusion | flops 14680064 | bytes 25165824 | tf_op jit(solution)/shard_map/add | solution.py:93
  361.8 6.5 %pad_maximum_fusion = f32[2048,1024]{0,1:T(8,128)} fusion(f32[2048,512]{0,1:T(8,128)} %get-tuple-element.51, f32[2048,512]{0,1:T(8,128)S(1)} %get-tuple-element.50), kind=kLoop, calls=%fused_computation.16 | loop fusion | flops 2097152 | bytes 16777216 | tf_op jit(solution)/shard_map/concatenate | solution.py:93
  369.9 14.6 %fusion.144 = bf16[8,128,128]{1,2,0:T(8,128)(2,1)S(1)} fusion(f32[2048,128,8]{1,0,2:T(8,128)} %fusion.174, bf16[2048,512]{1,0:T(8,128)(2,1)S(1)} %copy-done.17, f32[8,128,2048]{1,2,0:T(8,128)} %get-tuple-element.43, f32[8,128]{1,0:T(8,128)S(1)} %copy-done.19), kind=kOutput, calls=%fused_computation.171 | convolution fusion | flops 551685120 | bytes 34349056 | tf_op jit(solution)/shard_map/htk,kd->thd/dot_general | solution.py:35
  384.7 14.8 %fusion.146 = bf16[8,128,128]{1,2,0:T(8,128)(2,1)S(1)} fusion(f32[2048,128,8]{1,0,2:T(8,128)} %fusion.170, bf16[2048,512]{1,0:T(8,128)(2,1)S(1)} %copy-done.17, f32[8,128,2048]{1,2,0:T(8,128)} %get-tuple-element.47, f32[8,128]{1,0:T(8,128)S(1)} %copy-done.21), kind=kOutput, calls=%fused_computation.173 | convolution fusion | flops 551685120 | bytes 34349056 | tf_op jit(solution)/shard_map/htk,kd->thd/dot_general | solution.py:35
  399.7 13.8 %fusion.145 = bf16[8,128,128]{1,2,0:T(8,128)(2,1)S(1)} fusion(f32[2048,128,8]{1,0,2:T(8,128)} %fusion.172, bf16[2048,512]{1,0:T(8,128)(2,1)S(1)} %copy-done.17, f32[8,128,2048]{1,2,0:T(8,128)} %get-tuple-element.45, f32[8,128]{1,0:T(8,128)S(1)} %copy-done.23), kind=kOutput, calls=%fused_computation.172 | convolution fusion | flops 551685120 | bytes 34349056 | tf_op jit(solution)/shard_map/htk,kd->thd/dot_general | solution.py:35
  413.7 13.5 %fusion.147 = bf16[8,128,128]{1,2,0:T(8,128)(2,1)S(1)} fusion(f32[2048,128,8]{1,0,2:T(8,128)} %fusion.168, bf16[2048,512]{1,0:T(8,128)(2,1)S(1)} %copy-done.17, f32[8,128,2048]{1,2,0:T(8,128)} %get-tuple-element.49, f32[8,128]{1,0:T(8,128)S(1)} %copy-done.25), kind=kOutput, calls=%fused_computation.174 | convolution fusion | flops 551685120 | bytes 34349056 | tf_op jit(solution)/shard_map/htk,kd->thd/dot_general | solution.py:35
  427.3 13.5 %fusion.148 = bf16[8,128,128]{1,2,0:T(8,128)(2,1)S(1)} fusion(f32[2048,128,8]{1,0,2:T(8,128)} %fusion.175, bf16[2048,512]{1,0:T(8,128)(2,1)} %all-gather.3.cloned.1.call-done, f32[8,128,2048]{1,2,0:T(8,128)} %get-tuple-element.35, f32[8,128]{1,0:T(8,128)S(1)} %copy-done.27), kind=kOutput, calls=%fused_computation.175 | convolution fusion | flops 551685120 | bytes 34349056 | tf_op jit(solution)/shard_map/htk,kd->thd/dot_general | solution.py:35
  441.0 13.4 %fusion.150 = bf16[8,128,128]{1,2,0:T(8,128)(2,1)S(1)} fusion(f32[2048,128,8]{1,0,2:T(8,128)} %fusion.171, bf16[2048,512]{1,0:T(8,128)(2,1)} %all-gather.3.cloned.1.call-done, f32[8,128,2048]{1,2,0:T(8,128)} %get-tuple-element.39, f32[8,128]{1,0:T(8,128)S(1)} %get-tuple-element.38), kind=kOutput, calls=%fused_computation.177 | convolution fusion | flops 551685120 | bytes 34349056 | tf_op jit(solution)/shard_map/htk,kd->thd/dot_general | solution.py:35
  454.6 13.4 %fusion.149 = bf16[8,128,128]{1,2,0:T(8,128)(2,1)S(1)} fusion(f32[2048,128,8]{1,0,2:T(8,128)} %fusion.173, bf16[2048,512]{1,0:T(8,128)(2,1)} %all-gather.3.cloned.1.call-done, f32[8,128,2048]{1,2,0:T(8,128)} %get-tuple-element.37, f32[8,128]{1,0:T(8,128)S(1)} %get-tuple-element.36), kind=kOutput, calls=%fused_computation.176 | convolution fusion | flops 551685120 | bytes 34349056 | tf_op jit(solution)/shard_map/htk,kd->thd/dot_general | solution.py:35
  468.1 13.1 %fusion.151 = bf16[8,128,128]{1,2,0:T(8,128)(2,1)S(1)} fusion(f32[2048,128,8]{1,0,2:T(8,128)} %fusion.169, bf16[2048,512]{1,0:T(8,128)(2,1)} %all-gather.3.cloned.1.call-done, f32[8,128,2048]{1,2,0:T(8,128)} %get-tuple-element.41, f32[8,128]{1,0:T(8,128)S(1)} %get-tuple-element.40), kind=kOutput, calls=%fused_computation.178 | convolution fusion | flops 551685120 | bytes 34349056 | tf_op jit(solution)/shard_map/htk,kd->thd/dot_general | solution.py:35
  (116 shorter events, 84.2 us)
Async XLA Ops:
  7.2 12.1 %copy-start.6 = (bf16[128,4096]{1,0:T(8,128)(2,1)S(1)}, bf16[128,4096]{1,0:T(8,128)(2,1)}, u32[]{:S(2)}) copy-start(bf16[128,4096]{1,0:T(8,128)(2,1)} %param.12) | copy-start | bytes 3145732
  7.2 14.9 %copy-start.7 = (bf16[128,4096]{1,0:T(8,128)(2,1)S(1)}, bf16[128,4096]{1,0:T(8,128)(2,1)}, u32[]{:S(2)}) copy-start(bf16[128,4096]{1,0:T(8,128)(2,1)} %param.13) | copy-start | bytes 3145732
  7.2 54.6 %all-gather.3.cloned.1.call-start = ((), (), s32[]{:S(2)}) async-start(), calls=%async_computation.1 | async-start | bytes 2228224 | tf_op jit(solution)/shard_map/all_gather | solution.py:72
  7.9 102.7 %all-gather.5.cloned.1.call-start = ((), (), s32[]{:S(2)}) async-start(), calls=%async_computation.2 | async-start | bytes 2228224 | tf_op jit(solution)/shard_map/all_gather | solution.py:73
  8.7 474.2 %reduce-scatter.2.cloned.1.call-start = ((), (), s32[]{:S(2)}) async-start(), calls=%async_computation.3 | async-start | bytes 8912896 | tf_op jit(solution)/shard_map/reduce_scatter | solution.py:94
  24.2 106.4 %copy-start.12 = (pred[128,2048]{0,1:T(8,128)(4,1)}, pred[128,2048]{0,1:T(8,128)(4,1)S(1)}, u32[]{:S(2)}) copy-start(pred[128,2048]{0,1:T(8,128)(4,1)S(1)} %compare_and_fusion) | copy-start | bytes 786436
  68.9 47.2 %copy-start.18 = (f32[8,128]{1,0:T(8,128)}, f32[8,128]{1,0:T(8,128)S(1)}, u32[]{:S(2)}) copy-start(f32[8,128]{1,0:T(8,128)S(1)} %get-tuple-element.42) | copy-start | bytes 12292
  74.8 41.3 %copy-start.16 = (bf16[128,1024]{0,1:T(8,128)(2,1)S(1)}, bf16[128,1024]{0,1:T(8,128)(2,1)}, u32[]{:S(2)}) copy-start(bf16[128,1024]{0,1:T(8,128)(2,1)} %copy.288) | copy-start | bytes 786436
  116.1 14.5 %copy-start.15 = (bf16[128,1024]{0,1:T(8,128)(2,1)S(1)}, bf16[128,1024]{0,1:T(8,128)(2,1)}, u32[]{:S(2)}) copy-start(bf16[128,1024]{0,1:T(8,128)(2,1)} %copy.284) | copy-start | bytes 786436
  137.7 10.5 %copy-start.20 = (f32[8,128]{1,0:T(8,128)}, f32[8,128]{1,0:T(8,128)S(1)}, u32[]{:S(2)}) copy-start(f32[8,128]{1,0:T(8,128)S(1)} %get-tuple-element.46) | copy-start | bytes 12292
  137.7 6.0 %copy-start = (bf16[2048,512]{1,0:T(8,128)(2,1)S(1)}, bf16[2048,512]{1,0:T(8,128)(2,1)}, u32[]{:S(2)}) copy-start(bf16[2048,512]{1,0:T(8,128)(2,1)} %all-gather.5.cloned.1.call-done) | copy-start | bytes 6291460
  148.1 14.2 %copy-start.13 = (pred[128,2048]{0,1:T(8,128)(4,1)S(1)}, pred[128,2048]{0,1:T(8,128)(4,1)}, u32[]{:S(2)}) copy-start(pred[128,2048]{0,1:T(8,128)(4,1)} %copy-done.12) | copy-start | bytes 786436
  169.4 10.5 %copy-start.22 = (f32[8,128]{1,0:T(8,128)}, f32[8,128]{1,0:T(8,128)S(1)}, u32[]{:S(2)}) copy-start(f32[8,128]{1,0:T(8,128)S(1)} %get-tuple-element.44) | copy-start | bytes 12292
  179.9 14.2 %copy-start.11 = (bf16[128,1024]{0,1:T(8,128)(2,1)S(1)}, bf16[128,1024]{0,1:T(8,128)(2,1)}, u32[]{:S(2)}) copy-start(bf16[128,1024]{0,1:T(8,128)(2,1)} %copy.282) | copy-start | bytes 786436
  201.1 10.3 %copy-start.24 = (f32[8,128]{1,0:T(8,128)}, f32[8,128]{1,0:T(8,128)S(1)}, u32[]{:S(2)}) copy-start(f32[8,128]{1,0:T(8,128)S(1)} %get-tuple-element.48) | copy-start | bytes 12292
  233.2 10.4 %copy-start.26 = (f32[8,128]{1,0:T(8,128)}, f32[8,128]{1,0:T(8,128)S(1)}, u32[]{:S(2)}) copy-start(f32[8,128]{1,0:T(8,128)S(1)} %get-tuple-element.34) | copy-start | bytes 12292
  243.6 14.4 %copy-start.10 = (bf16[128,1024]{0,1:T(8,128)(2,1)S(1)}, bf16[128,1024]{0,1:T(8,128)(2,1)}, u32[]{:S(2)}) copy-start(bf16[128,1024]{0,1:T(8,128)(2,1)} %copy.276) | copy-start | bytes 786436
  258.0 7.0 %copy-start.3 = (bf16[128,1024]{0,1:T(8,128)(2,1)S(1)}, bf16[128,1024]{0,1:T(8,128)(2,1)}, u32[]{:S(2)}) copy-start(bf16[128,1024]{0,1:T(8,128)(2,1)} %copy.277) | copy-start | bytes 786436
  275.5 14.6 %copy-start.9 = (bf16[128,1024]{0,1:T(8,128)(2,1)S(1)}, bf16[128,1024]{0,1:T(8,128)(2,1)}, u32[]{:S(2)}) copy-start(bf16[128,1024]{0,1:T(8,128)(2,1)} %copy.278) | copy-start | bytes 786436
  290.0 7.1 %copy-start.2 = (bf16[128,1024]{0,1:T(8,128)(2,1)S(1)}, bf16[128,1024]{0,1:T(8,128)(2,1)}, u32[]{:S(2)}) copy-start(bf16[128,1024]{0,1:T(8,128)(2,1)} %copy.279) | copy-start | bytes 786436
  307.5 14.3 %copy-start.8 = (bf16[128,1024]{0,1:T(8,128)(2,1)S(1)}, bf16[128,1024]{0,1:T(8,128)(2,1)}, u32[]{:S(2)}) copy-start(bf16[128,1024]{0,1:T(8,128)(2,1)} %copy.274) | copy-start | bytes 786436
  307.5 14.3 %copy-start.14 = (pred[128,2048]{0,1:T(8,128)(4,1)S(1)}, pred[128,2048]{0,1:T(8,128)(4,1)}, u32[]{:S(2)}) copy-start(pred[128,2048]{0,1:T(8,128)(4,1)} %copy-done.12) | copy-start | bytes 786436
  321.9 7.1 %copy-start.1 = (bf16[128,1024]{0,1:T(8,128)(2,1)S(1)}, bf16[128,1024]{0,1:T(8,128)(2,1)}, u32[]{:S(2)}) copy-start(bf16[128,1024]{0,1:T(8,128)(2,1)} %copy.275) | copy-start | bytes 786436
  339.3 14.4 %copy-start.4 = (f32[2048,128]{0,1:T(8,128)S(1)}, f32[2048,128]{0,1:T(8,128)}, u32[]{:S(2)}) copy-start(f32[2048,128]{0,1:T(8,128)} %fusion.141) | copy-start | bytes 3145732
  339.3 14.4 %copy-start.5 = (f32[2048,128]{0,1:T(8,128)S(1)}, f32[2048,128]{0,1:T(8,128)}, u32[]{:S(2)}) copy-start(f32[2048,128]{0,1:T(8,128)} %fusion.112) | copy-start | bytes 3145732
  368.3 1.6 copy-start.17
  368.3 1.6 copy-start.19
  369.9 14.8 %copy-start.21 = (f32[8,128]{1,0:T(8,128)S(1)}, f32[8,128]{1,0:T(8,128)}, u32[]{:S(2)}) copy-start(f32[8,128]{1,0:T(8,128)} %copy-done.20) | copy-start | bytes 12292
  384.7 15.0 %copy-start.23 = (f32[8,128]{1,0:T(8,128)S(1)}, f32[8,128]{1,0:T(8,128)}, u32[]{:S(2)}) copy-start(f32[8,128]{1,0:T(8,128)} %copy-done.22) | copy-start | bytes 12292
  399.7 13.9 %copy-start.25 = (f32[8,128]{1,0:T(8,128)S(1)}, f32[8,128]{1,0:T(8,128)}, u32[]{:S(2)}) copy-start(f32[8,128]{1,0:T(8,128)} %copy-done.24) | copy-start | bytes 12292
  413.6 13.6 %copy-start.27 = (f32[8,128]{1,0:T(8,128)S(1)}, f32[8,128]{1,0:T(8,128)}, u32[]{:S(2)}) copy-start(f32[8,128]{1,0:T(8,128)} %copy-done.26) | copy-start | bytes 12292
Sparse Core Ops, SparseCore 0:
  10.5 51.2 all-gather.2
  64.3 46.3 all-gather.4
  368.5 99.8 reduce-scatter.1
where the time goes:
time: 500 us; the launch traced here: 492 us
  matrix products  366 us (73%)
  waiting for transfers between devices  74.8 us (15%)
  other arithmetic  20.2 us (4%)
  local copies, waits for them, and re-layouts  16.7 us (3%)
  between operations  14.3 us (3%)
    dot_general x8, matrix products, head_group(): jnp.einsum('htk,thd->kd', dscores_low, query_block, preferred_element_typ...  115 us
    dot_general x8, matrix products, head_group(): jnp.einsum('htk,kd->thd', dscores_low, key_block, preferred_element_type=...  110 us
    sub x8, matrix products, head_group(): expo = jnp.exp(scores - peak)  56.5 us
    dot_general x8, matrix products, head_group(): jnp.einsum('htk,thd->kd', probs_low, cot_block, preferred_element_type=jn...  47.3 us
    all_gather x1, waiting for transfers between devices, local(): lax.all_gather(shared_keys, 'ctx', axis=0, tiled=True)  37.6 us
    dot_general x8, matrix products, head_group(): jnp.einsum('thd,kd->htk', cot_block, value_block, preferred_element_type=...  36.9 us
    all_gather x1, waiting for transfers between devices, local(): lax.all_gather(common_values, 'ctx', axis=0, tiled=True)  35.8 us
    unnamed x74, local copies, waits for them, and re-layouts  12.7 us
  transfers between devices with their start and end apart: 3, of which 2 were waited for; matrix products, arithmetic and copies ran while one was open for 29% of the time, Pallas kernels for 0%

commit v1 on v0

--- a/solution.py
+++ b/solution.py
@@ -69,7 +69,9 @@
     lengths,
 ):
     all_keys, all_values = (
-        lax.all_gather(shared_keys, "ctx", axis=0, tiled=True),
+        jnp.concatenate(
+            lax.all_to_all(jnp.stack([shared_keys] * lax.axis_size("ctx")), "ctx", 0, 0), axis=0
+        ),
         lax.all_gather(common_values, "ctx", axis=0, tiled=True),
     )
     rows_here = query_one.shape[0]

time: 500 us -> 441 us (0.88)
  waiting for transfers between devices: 74.8 us -> 0.7 us
  local copies, waits for them, and re-layouts: 16.7 us -> 38.7 us
  matrix products: 366 us -> 352 us
  starting transfers between devices: 0.11 us -> 9.55 us
    all_gather x1 -> x0, waiting for transfers between devices: 37.6 us -> none  [local(): lax.all_gather(shared_keys, 'ctx', axis=0, tiled=True)]
    all_gather x1, waiting for transfers between devices: 35.8 us -> 0.01 us  [local(): lax.all_gather(common_values, 'ctx', axis=0, tiled=True)]
    dot_general x8, matrix products: 47.3 us -> 30.6 us  [head_group(): jnp.einsum('htk,thd->kd', probs_low, cot_block, preferred_element_type=jn...]
    unnamed x74 -> x68, local copies, waits for them, and re-layouts: 12.7 us -> 23.4 us
    all_to_all x0 -> x1, starting transfers between devices: none -> 9.47 us  [local(): lax.all_to_all(jnp.stack([shared_keys] * lax.axis_size('ctx')), 'ctx', 0, 0)]
    reshape x8, local copies, waits for them, and re-layouts: 1.16 us -> 6.32 us  [head_group(): query_part = jnp.einsum('htk,kd->thd', dscores_low, key_block, preferred_...]
  transfers between devices with their start and end apart: 3 -> 3, of which waited for: 2 -> 0; matrix products, arithmetic and copies ran while one was open for 29% -> 55% of each run, Pallas kernels for 0% -> 0%
where the time goes in v1:
time: 441 us; the launch traced here: 437 us
  matrix products  352 us (80%)
  local copies, waits for them, and re-layouts  38.7 us (9%)
  other arithmetic  22.3 us (5%)
  between operations  14.5 us (3%)
  starting transfers between devices  9.55 us (2%)
    dot_general x8, matrix products, head_group(): jnp.einsum('htk,thd->kd', dscores_low, query_block, preferred_element_typ...  114 us
    dot_general x8, matrix products, head_group(): jnp.einsum('htk,kd->thd', dscores_low, key_block, preferred_element_type=...  113 us
    sub x8, matrix products, head_group(): expo = jnp.exp(scores - peak)  57.1 us
    dot_general x8, matrix products, head_group(): jnp.einsum('thd,kd->htk', cot_block, value_block, preferred_element_type=...  36.8 us
    dot_general x8, matrix products, head_group(): jnp.einsum('htk,thd->kd', probs_low, cot_block, preferred_element_type=jn...  30.6 us
    unnamed x68, local copies, waits for them, and re-layouts  23.4 us
    all_to_all x1, starting transfers between devices, local(): lax.all_to_all(jnp.stack([shared_keys] * lax.axis_size('ctx')), 'ctx', 0, 0)  9.47 us
  transfers between devices with their start and end apart: 3, of which 0 were waited for; matrix products, arithmetic and copies ran while one was open for 55% of the time, Pallas kernels for 0%

profile of v1, /device:TPU:1, one launch (start us, length us, event | category | flops | bytes accessed | tf_op | source)
XLA Modules:
  0.0 437.3 jit_solution(4462275549331445816)
XLA Ops:
  10.4 9.5 %all-to-all-start = ((bf16[16,128,512]{2,1,0:T(8,128)(2,1)}), bf16[16,128,512]{2,1,0:T(8,128)(2,1)S(1)}, u32[]{:S(2)}, u32[]{:S(2)}) async-start(bf16[16,128,512]{2,1,0:T(8,128)(2,1)} %stack.2), calls=%async_computation | async-start | bytes 4194304 | tf_op jit(solution)/shard_map/all_to_all | solution.py:73
  50.3 7.4 %fusion.242 = (f32[8,128]{1,0:T(8,128)S(1)}, f32[8,128,2048]{1,2,0:T(8,128)}) fusion(pred[128,2048]{0,1:T(8,128)(4,1)} %compare_and_fusion, bf16[128,8,128]{0,2,1:T(8,128)(2,1)} %bitcast.577, bf16[2048,512]{1,0:T(8,128)(2,1)S(1)} %bitcast.531), kind=kOutput, calls=%fused_computation.279 | convolution fusion | flops 545261568 | bytes 9441280 | tf_op jit(solution)/shard_map/sub | solution.py:29
  57.6 7.0 %fusion.238 = (f32[8,128]{1,0:T(8,128)S(1)}, f32[8,128,2048]{1,2,0:T(8,128)}) fusion(pred[128,2048]{0,1:T(8,128)(4,1)} %compare_and_fusion, bf16[128,8,128]{0,2,1:T(8,128)(2,1)} %bitcast.571, bf16[2048,512]{1,0:T(8,128)(2,1)S(1)} %bitcast.532), kind=kOutput, calls=%fused_computation.275 | convolution fusion | flops 545261568 | bytes 9441280 | tf_op jit(solution)/shard_map/sub | solution.py:29
  64.7 7.0 %fusion.243 = (f32[8,128]{1,0:T(8,128)S(1)}, f32[8,128,2048]{1,2,0:T(8,128)}) fusion(pred[128,2048]{0,1:T(8,128)(4,1)} %compare_and_fusion, bf16[128,8,128]{0,2,1:T(8,128)(2,1)} %bitcast.575, bf16[2048,512]{1,0:T(8,128)(2,1)S(1)} %bitcast.533), kind=kOutput, calls=%fused_computation.280 | convolution fusion | flops 545261568 | bytes 9441280 | tf_op jit(solution)/shard_map/sub | solution.py:29
  71.7 7.0 %fusion.239 = (f32[8,128]{1,0:T(8,128)S(1)}, f32[8,128,2048]{1,2,0:T(8,128)}) fusion(pred[128,2048]{0,1:T(8,128)(4,1)} %compare_and_fusion, bf16[128,8,128]{0,2,1:T(8,128)(2,1)} %bitcast.567, bf16[2048,512]{1,0:T(8,128)(2,1)S(1)} %bitcast.534), kind=kOutput, calls=%fused_computation.276 | convolution fusion | flops 545261568 | bytes 9441280 | tf_op jit(solution)/shard_map/sub | solution.py:29
  78.7 7.3 %fusion.241 = (f32[8,128]{1,0:T(8,128)S(1)}, f32[8,128,2048]{1,2,0:T(8,128)}) fusion(pred[128,2048]{0,1:T(8,128)(4,1)} %compare_and_fusion, bf16[128,8,128]{0,2,1:T(8,128)(2,1)} %bitcast.573, bf16[2048,512]{1,0:T(8,128)(2,1)S(1)} %bitcast.535), kind=kOutput, calls=%fused_computation.278 | convolution fusion | flops 545261568 | bytes 9441280 | tf_op jit(solution)/shard_map/sub | solution.py:29
  86.0 7.0 %fusion.244 = (f32[8,128]{1,0:T(8,128)S(1)}, f32[8,128,2048]{1,2,0:T(8,128)}) fusion(pred[128,2048]{0,1:T(8,128)(4,1)} %compare_and_fusion, bf16[128,8,128]{0,2,1:T(8,128)(2,1)} %bitcast.569, bf16[2048,512]{1,0:T(8,128)(2,1)S(1)} %bitcast.536), kind=kOutput, calls=%fused_computation.281 | convolution fusion | flops 545261568 | bytes 9441280 | tf_op jit(solution)/shard_map/sub | solution.py:29
  93.0 6.0 %fusion.138 = f32[2048,128]{0,1:T(8,128)} fusion(bf16[128,8,128]{0,2,1:T(8,128)(2,1)} %bitcast.561, f32[8,128,2048]{1,2,0:T(8,128)} %get-tuple-element.45, f32[8,128]{1,0:T(8,128)S(1)} %get-tuple-element.44), kind=kOutput, calls=%fused_computation.169 | convolution fusion | flops 541065216 | bytes 9703424 | tf_op jit(solution)/shard_map/htk,thd->kd/dot_general | solution.py:41
  99.0 6.0 %fusion.126 = f32[2048,128]{0,1:T(8,128)} fusion(bf16[128,8,128]{0,2,1:T(8,128)(2,1)S(1)} %bitcast.555, f32[8,128,2048]{1,2,0:T(8,128)} %get-tuple-element.37, f32[8,128]{1,0:T(8,128)S(1)} %get-tuple-element.36), kind=kOutput, calls=%fused_computation.165 | convolution fusion | flops 541065216 | bytes 9703424 | tf_op jit(solution)/shard_map/htk,thd->kd/dot_general | solution.py:41
  112.9 7.4 %fusion.240 = (f32[8,128]{1,0:T(8,128)S(1)}, f32[8,128,2048]{1,2,0:T(8,128)}) fusion(pred[128,2048]{0,1:T(8,128)(4,1)} %compare_and_fusion, bf16[128,8,128]{0,2,1:T(8,128)(2,1)} %bitcast.563, bf16[2048,512]{1,0:T(8,128)(2,1)S(1)} %bitcast.537), kind=kOutput, calls=%fused_computation.277 | convolution fusion | flops 545261568 | bytes 9441280 | tf_op jit(solution)/shard_map/sub | solution.py:29
  120.3 7.0 %fusion.237 = (f32[8,128]{1,0:T(8,128)S(1)}, f32[8,128,2048]{1,2,0:T(8,128)}) fusion(pred[128,2048]{0,1:T(8,128)(4,1)} %compare_and_fusion, bf16[128,8,128]{0,2,1:T(8,128)(2,1)} %bitcast.565, bf16[2048,512]{1,0:T(8,128)(2,1)S(1)} %bitcast.538), kind=kOutput, calls=%fused_computation.274 | convolution fusion | flops 545261568 | bytes 9441280 | tf_op jit(solution)/shard_map/sub | solution.py:29
  127.3 6.0 %fusion.132 = f32[2048,128]{0,1:T(8,128)} fusion(bf16[128,8,128]{0,2,1:T(8,128)(2,1)S(1)} %bitcast.553, f32[8,128,2048]{1,2,0:T(8,128)} %get-tuple-element.49, f32[8,128]{1,0:T(8,128)S(1)} %get-tuple-element.48), kind=kOutput, calls=%fused_computation.167 | convolution fusion | flops 541065216 | bytes 9703424 | tf_op jit(solution)/shard_map/htk,thd->kd/dot_general | solution.py:41
  138.6 5.5 %fusion.172 = f32[2048,128,8]{1,0,2:T(8,128)} fusion(bf16[128,8,128]{0,2,1:T(8,128)(2,1)S(1)} %bitcast.562, bf16[2048,512]{1,0:T(8,128)(2,1)} %all-gather.2.cloned.1.call-done), kind=kOutput, calls=%fused_computation.202 | convolution fusion | flops 536870912 | bytes 9175040 | tf_op jit(solution)/shard_map/thd,kd->htk/dot_general | solution.py:32
  144.1 14.3 %fusion.113 = f32[2048,128]{0,1:T(8,128)} fusion(bf16[128,8,128]{0,2,1:T(8,128)(2,1)} %bitcast.578, f32[2048,128,8]{1,0,2:T(8,128)} %fusion.172, f32[8,128,2048]{1,2,0:T(8,128)} %get-tuple-element.45, f32[8,128]{1,0:T(8,128)S(1)} %get-tuple-element.44), kind=kOutput, calls=%fused_computation.156 | convolution fusion | flops 551554048 | bytes 18092032 | tf_op jit(solution)/shard_map/htk,thd->kd/dot_general | solution.py:38
  162.9 14.3 %fusion.117 = f32[2048,128]{0,1:T(8,128)} fusion(bf16[128,8,128]{0,2,1:T(8,128)(2,1)} %bitcast.572, f32[2048,128,8]{1,0,2:T(8,128)} %fusion.173, f32[8,128,2048]{1,2,0:T(8,128)} %get-tuple-element.37, f32[8,128]{1,0:T(8,128)S(1)} %get-tuple-element.36), kind=kOutput, calls=%fused_computation.160 | convolution fusion | flops 551554048 | bytes 18092032 | tf_op jit(solution)/shard_map/htk,thd->kd/dot_general | solution.py:38
  181.6 14.2 %fusion.114 = f32[2048,128]{0,1:T(8,128)} fusion(bf16[128,8,128]{0,2,1:T(8,128)(2,1)} %bitcast.576, f32[2048,128,8]{1,0,2:T(8,128)} %fusion.170, f32[8,128,2048]{1,2,0:T(8,128)} %get-tuple-element.47, f32[8,128]{1,0:T(8,128)S(1)} %get-tuple-element.46), kind=kOutput, calls=%fused_computation.157 | convolution fusion | flops 551554048 | bytes 18092032 | tf_op jit(solution)/shard_map/htk,thd->kd/dot_general | solution.py:38
  200.3 14.0 %fusion.118 = f32[2048,128]{0,1:T(8,128)} fusion(bf16[128,8,128]{0,2,1:T(8,128)(2,1)S(1)} %bitcast.568, f32[2048,128,8]{1,0,2:T(8,128)} %fusion.171, f32[8,128,2048]{1,2,0:T(8,128)} %get-tuple-element.39, f32[8,128]{1,0:T(8,128)S(1)} %get-tuple-element.38), kind=kOutput, calls=%fused_computation.161 | convolution fusion | flops 551554048 | bytes 18092032 | tf_op jit(solution)/shard_map/htk,thd->kd/dot_general | solution.py:38
  214.4 4.5 %fusion.174 = f32[2048,128,8]{1,0,2:T(8,128)} fusion(bf16[128,8,128]{0,2,1:T(8,128)(2,1)S(1)} %bitcast.558, bf16[2048,512]{1,0:T(8,128)(2,1)S(1)} %copy-done), kind=kOutput, calls=%fused_computation.204 | convolution fusion | flops 536870912 | bytes 9175040 | tf_op jit(solution)/shard_map/thd,kd->htk/dot_general | solution.py:32
  218.9 14.5 %fusion.112 = f32[2048,128]{0,1:T(8,128)} fusion(bf16[128,8,128]{0,2,1:T(8,128)(2,1)S(1)} %bitcast.574, f32[2048,128,8]{1,0,2:T(8,128)} %fusion.174, f32[8,128,2048]{1,2,0:T(8,128)} %get-tuple-element.43, f32[8,128]{1,0:T(8,128)S(1)} %get-tuple-element.42), kind=kOutput, calls=%fused_computation.155 | convolution fusion | flops 551554048 | bytes 18092032 | tf_op jit(solution)/shard_map/htk,thd->kd/dot_general | solution.py:38
  237.9 14.6 %fusion.115 = f32[2048,128]{0,1:T(8,128)} fusion(bf16[128,8,128]{0,2,1:T(8,128)(2,1)S(1)} %bitcast.570, f32[2048,128,8]{1,0,2:T(8,128)} %fusion.168, f32[8,128,2048]{1,2,0:T(8,128)} %get-tuple-element.49, f32[8,128]{1,0:T(8,128)S(1)} %get-tuple-element.48), kind=kOutput, calls=%fused_computation.158 | convolution fusion | flops 551554048 | bytes 18092032 | tf_op jit(solution)/shard_map/htk,thd->kd/dot_general | solution.py:38
  256.9 14.0 %fusion.119 = f32[2048,128]{0,1:T(8,128)} fusion(bf16[128,8,128]{0,2,1:T(8,128)(2,1)S(1)} %bitcast.564, f32[2048,128,8]{1,0,2:T(8,128)} %fusion.169, f32[8,128,2048]{1,2,0:T(8,128)} %get-tuple-element.41, f32[8,128]{1,0:T(8,128)S(1)} %get-tuple-element.40), kind=kOutput, calls=%fused_computation.162 | convolution fusion | flops 551554048 | bytes 18092032 | tf_op jit(solution)/shard_map/htk,thd->kd/dot_general | solution.py:38
  275.4 14.5 %fusion.116 = f32[2048,128]{0,1:T(8,128)} fusion(bf16[128,8,128]{0,2,1:T(8,128)(2,1)S(1)} %bitcast.566, f32[2048,128,8]{1,0,2:T(8,128)} %fusion.175, f32[8,128,2048]{1,2,0:T(8,128)} %get-tuple-element.35, f32[8,128]{1,0:T(8,128)S(1)} %get-tuple-element.34), kind=kOutput, calls=%fused_computation.159 | convolution fusion | flops 551554048 | bytes 18092032 | tf_op jit(solution)/shard_map/htk,thd->kd/dot_general | solution.py:38
  289.8 8.3 %maximum_add_fusion = (f32[2048,512]{0,1:T(8,128)S(1)}, f32[2048,512]{0,1:T(8,128)}) fusion(f32[2048,128]{0,1:T(8,128)} %fusion.116, f32[2048,128]{0,1:T(8,128)} %fusion.117, f32[2048,128]{0,1:T(8,128)} %fusion.118, f32[2048,128]{0,1:T(8,128)} %fusion.119, f32[2048,128]{0,1:T(8,128)} %fusion.112, f32[2048,128]{0,1:T(8,128)} %fusion.113, ...), kind=kLoop, calls=%fused_computation.81 | loop fusion | flops 14680064 | bytes 25165824 | tf_op jit(solution)/shard_map/add | solution.py:95
  298.1 6.5 %pad_maximum_fusion = f32[2048,1024]{0,1:T(8,128)} fusion(f32[2048,512]{0,1:T(8,128)} %get-tuple-element.51, f32[2048,512]{0,1:T(8,128)S(1)} %get-tuple-element.50), kind=kLoop, calls=%fused_computation.16 | loop fusion | flops 2097152 | bytes 16777216 | tf_op jit(solution)/shard_map/concatenate | solution.py:95
  306.2 13.7 %fusion.145 = bf16[8,128,128]{1,2,0:T(8,128)(2,1)S(1)} fusion(f32[2048,128,8]{1,0,2:T(8,128)} %fusion.172, bf16[2048,512]{1,0:T(8,128)(2,1)S(1)} %bitcast.539, f32[8,128,2048]{1,2,0:T(8,128)} %get-tuple-element.45, f32[8,128]{1,0:T(8,128)S(1)} %get-tuple-element.44), kind=kOutput, calls=%fused_computation.172 | convolution fusion | flops 551685120 | bytes 34349056 | tf_op jit(solution)/shard_map/htk,kd->thd/dot_general | solution.py:35
  320.1 15.7 %fusion.149 = bf16[8,128,128]{1,2,0:T(8,128)(2,1)S(1)} fusion(f32[2048,128,8]{1,0,2:T(8,128)} %fusion.173, bf16[2048,512]{1,0:T(8,128)(2,1)S(1)} %bitcast.540, f32[8,128,2048]{1,2,0:T(8,128)} %get-tuple-element.37, f32[8,128]{1,0:T(8,128)S(1)} %get-tuple-element.36), kind=kOutput, calls=%fused_computation.176 | convolution fusion | flops 551685120 | bytes 34349056 | tf_op jit(solution)/shard_map/htk,kd->thd/dot_general | solution.py:35
  336.0 13.8 %fusion.146 = bf16[8,128,128]{1,2,0:T(8,128)(2,1)S(1)} fusion(f32[2048,128,8]{1,0,2:T(8,128)} %fusion.170, bf16[2048,512]{1,0:T(8,128)(2,1)S(1)} %bitcast.541, f32[8,128,2048]{1,2,0:T(8,128)} %get-tuple-element.47, f32[8,128]{1,0:T(8,128)S(1)} %get-tuple-element.46), kind=kOutput, calls=%fused_computation.173 | convolution fusion | flops 551685120 | bytes 34349056 | tf_op jit(solution)/shard_map/htk,kd->thd/dot_general | solution.py:35
  349.9 13.4 %fusion.150 = bf16[8,128,128]{1,2,0:T(8,128)(2,1)S(1)} fusion(f32[2048,128,8]{1,0,2:T(8,128)} %fusion.171, bf16[2048,512]{1,0:T(8,128)(2,1)S(1)} %bitcast.542, f32[8,128,2048]{1,2,0:T(8,128)} %get-tuple-element.39, f32[8,128]{1,0:T(8,128)S(1)} %get-tuple-element.38), kind=kOutput, calls=%fused_computation.177 | convolution fusion | flops 551685120 | bytes 34349056 | tf_op jit(solution)/shard_map/htk,kd->thd/dot_general | solution.py:35
  363.5 14.4 %fusion.144 = bf16[8,128,128]{1,2,0:T(8,128)(2,1)} fusion(f32[2048,128,8]{1,0,2:T(8,128)} %fusion.174, bf16[2048,512]{1,0:T(8,128)(2,1)S(1)} %bitcast.543, f32[8,128,2048]{1,2,0:T(8,128)} %get-tuple-element.43, f32[8,128]{1,0:T(8,128)S(1)} %get-tuple-element.42), kind=kOutput, calls=%fused_computation.171 | convolution fusion | flops 551685120 | bytes 34349056 | tf_op jit(solution)/shard_map/htk,kd->thd/dot_general | solution.py:35
  379.0 13.7 %fusion.147 = bf16[8,128,128]{1,2,0:T(8,128)(2,1)} fusion(f32[2048,128,8]{1,0,2:T(8,128)} %fusion.168, bf16[2048,512]{1,0:T(8,128)(2,1)S(1)} %bitcast.544, f32[8,128,2048]{1,2,0:T(8,128)} %get-tuple-element.49, f32[8,128]{1,0:T(8,128)S(1)} %get-tuple-element.48), kind=kOutput, calls=%fused_computation.174 | convolution fusion | flops 551685120 | bytes 34349056 | tf_op jit(solution)/shard_map/htk,kd->thd/dot_general | solution.py:35
  394.5 14.0 %fusion.151 = bf16[8,128,128]{1,2,0:T(8,128)(2,1)} fusion(f32[2048,128,8]{1,0,2:T(8,128)} %fusion.169, bf16[2048,512]{1,0:T(8,128)(2,1)S(1)} %bitcast.545, f32[8,128,2048]{1,2,0:T(8,128)} %get-tuple-element.41, f32[8,128]{1,0:T(8,128)S(1)} %get-tuple-element.40), kind=kOutput, calls=%fused_computation.178 | convolution fusion | flops 551685120 | bytes 34349056 | tf_op jit(solution)/shard_map/htk,kd->thd/dot_general | solution.py:35
  410.3 13.7 %fusion.148 = bf16[8,128,128]{1,2,0:T(8,128)(2,1)} fusion(f32[2048,128,8]{1,0,2:T(8,128)} %fusion.175, bf16[2048,512]{1,0:T(8,128)(2,1)S(1)} %bitcast.546, f32[8,128,2048]{1,2,0:T(8,128)} %get-tuple-element.35, f32[8,128]{1,0:T(8,128)S(1)} %get-tuple-element.34), kind=kOutput, calls=%fused_computation.175 | convolution fusion | flops 551685120 | bytes 34349056 | tf_op jit(solution)/shard_map/htk,kd->thd/dot_general | solution.py:35
  (114 shorter events, 86.5 us)
Async XLA Ops:
  7.2 23.0 %copy-start.10 = (bf16[128,4096]{1,0:T(8,128)(2,1)S(1)}, bf16[128,4096]{1,0:T(8,128)(2,1)}, u32[]{:S(2)}) copy-start(bf16[128,4096]{1,0:T(8,128)(2,1)} %param.9) | copy-start | bytes 3145732
  7.2 131.4 %all-gather.2.cloned.1.call-start = ((), (), s32[]{:S(2)}) async-start(), calls=%async_computation.2 | async-start | bytes 2228224 | tf_op jit(solution)/shard_map/all_gather | solution.py:75
  10.4 39.9 %all-to-all-start = ((bf16[16,128,512]{2,1,0:T(8,128)(2,1)}), bf16[16,128,512]{2,1,0:T(8,128)(2,1)S(1)}, u32[]{:S(2)}, u32[]{:S(2)}) async-start(bf16[16,128,512]{2,1,0:T(8,128)(2,1)} %stack.2), calls=%async_computation | async-start | bytes 4194304 | tf_op jit(solution)/shard_map/all_to_all | solution.py:73
  19.8 407.8 %reduce-scatter.2.cloned.1.call-start = ((), (), s32[]{:S(2)}) async-start(), calls=%async_computation.3 | async-start | bytes 8912896 | tf_op jit(solution)/shard_map/reduce_scatter | solution.py:96
  50.3 70.0 %copy-start.1 = (bf16[16,128,512]{2,1,0:T(8,128)(2,1)}, bf16[16,128,512]{2,1,0:T(8,128)(2,1)S(1)}, u32[]{:S(2)}) copy-start(bf16[16,128,512]{2,1,0:T(8,128)(2,1)S(1)} %all-to-all-done) | copy-start | bytes 6291460
  93.0 12.1 %slice-start.6 = ((s8[8388608]{0:T(1024)(128)(4,1)}), s8[4194304]{0:T(1024)(128)(4,1)S(1)}, s32[]{:S(2)}) async-start(s8[8388608]{0:T(1024)(128)(4,1)} %bitcast.595), calls=%async_computation.10 | async-start | bytes 8388608
  99.0 6.0 %slice-start.7 = ((s8[8388608]{0:T(1024)(128)(4,1)}), s8[4194304]{0:T(1024)(128)(4,1)S(1)}, s32[]{:S(2)}) async-start(s8[8388608]{0:T(1024)(128)(4,1)} %bitcast.595), calls=%async_computation.11 | async-start | bytes 8388608
  99.0 6.0 %copy-start.5 = (bf16[128,1024]{0,1:T(8,128)(2,1)S(1)}, bf16[128,1024]{0,1:T(8,128)(2,1)}, u32[]{:S(2)}) copy-start(bf16[128,1024]{0,1:T(8,128)(2,1)} %copy.285) | copy-start | bytes 786436
  99.0 8.6 %slice-start.4 = ((s8[8388608]{0:T(1024)(128)(4,1)}), s8[4194304]{0:T(1024)(128)(4,1)S(1)}, s32[]{:S(2)}) async-start(s8[8388608]{0:T(1024)(128)(4,1)} %bitcast.593), calls=%async_computation.8 | async-start | bytes 8388608
  105.1 2.6 slice-start.5
  105.1 5.1 %slice-start = ((s8[8388608]{0:T(1024)(128)(4,1)}), s8[4194304]{0:T(1024)(128)(4,1)S(1)}, s32[]{:S(2)}) async-start(s8[8388608]{0:T(1024)(128)(4,1)} %bitcast.589), calls=%async_computation.4 | async-start | bytes 8388608
  107.6 2.5 copy-start.3
  107.6 2.8 slice-start.1
  127.3 6.1 %copy-start.16 = (f32[8,128,2048]{1,2,0:T(8,128)S(1)}, f32[8,128,2048]{1,2,0:T(8,128)}, u32[]{:S(2)}) copy-start(f32[8,128,2048]{1,2,0:T(8,128)} %get-tuple-element.41) | copy-start | bytes 25165828
  127.3 8.5 %slice-start.2 = ((s8[8388608]{0:T(1024)(128)(4,1)}), s8[4194304]{0:T(1024)(128)(4,1)S(1)}, s32[]{:S(2)}) async-start(s8[8388608]{0:T(1024)(128)(4,1)} %bitcast.591), calls=%async_computation.6 | async-start | bytes 8388608
  133.4 2.7 slice-start.3
  136.1 2.5 copy-start.7
  144.1 14.3 %copy-start = (bf16[2048,512]{1,0:T(8,128)(2,1)S(1)}, bf16[2048,512]{1,0:T(8,128)(2,1)}, u32[]{:S(2)}) copy-start(bf16[2048,512]{1,0:T(8,128)(2,1)} %all-gather.2.cloned.1.call-done) | copy-start | bytes 6291460
  162.9 14.3 %copy-start.6 = (bf16[128,1024]{0,1:T(8,128)(2,1)S(1)}, bf16[128,1024]{0,1:T(8,128)(2,1)}, u32[]{:S(2)}) copy-start(bf16[128,1024]{0,1:T(8,128)(2,1)} %copy.285) | copy-start | bytes 786436
  195.8 4.5 %copy-start.13 = (bf16[128,1024]{0,1:T(8,128)(2,1)S(1)}, bf16[128,1024]{0,1:T(8,128)(2,1)}, u32[]{:S(2)}) copy-start(bf16[128,1024]{0,1:T(8,128)(2,1)} %copy.276) | copy-start | bytes 786436
  200.3 14.0 %copy-start.4 = (bf16[128,1024]{0,1:T(8,128)(2,1)S(1)}, bf16[128,1024]{0,1:T(8,128)(2,1)}, u32[]{:S(2)}) copy-start(bf16[128,1024]{0,1:T(8,128)(2,1)} %copy.289) | copy-start | bytes 786436
  214.3 4.5 %copy-start.15 = (bf16[128,1024]{0,1:T(8,128)(2,1)S(1)}, bf16[128,1024]{0,1:T(8,128)(2,1)}, u32[]{:S(2)}) copy-start(bf16[128,1024]{0,1:T(8,128)(2,1)} %copy.288) | copy-start | bytes 786436
  233.4 4.4 %copy-start.14 = (bf16[128,1024]{0,1:T(8,128)(2,1)S(1)}, bf16[128,1024]{0,1:T(8,128)(2,1)}, u32[]{:S(2)}) copy-start(bf16[128,1024]{0,1:T(8,128)(2,1)} %copy.282) | copy-start | bytes 786436
  252.4 4.5 %copy-start.11 = (bf16[128,1024]{0,1:T(8,128)(2,1)S(1)}, bf16[128,1024]{0,1:T(8,128)(2,1)}, u32[]{:S(2)}) copy-start(bf16[128,1024]{0,1:T(8,128)(2,1)} %copy.274) | copy-start | bytes 786436
  270.9 4.4 %copy-start.12 = (bf16[128,1024]{0,1:T(8,128)(2,1)S(1)}, bf16[128,1024]{0,1:T(8,128)(2,1)}, u32[]{:S(2)}) copy-start(bf16[128,1024]{0,1:T(8,128)(2,1)} %copy.280) | copy-start | bytes 786436
  275.4 14.5 %copy-start.8 = (f32[2048,128]{0,1:T(8,128)S(1)}, f32[2048,128]{0,1:T(8,128)}, u32[]{:S(2)}) copy-start(f32[2048,128]{0,1:T(8,128)} %fusion.138) | copy-start | bytes 3145732
  275.4 14.5 %copy-start.9 = (f32[2048,128]{0,1:T(8,128)S(1)}, f32[2048,128]{0,1:T(8,128)}, u32[]{:S(2)}) copy-start(f32[2048,128]{0,1:T(8,128)} %fusion.126) | copy-start | bytes 3145732
  304.6 1.6 copy-start.2
Sparse Core Ops, SparseCore 0:
  10.5 62.3 all-gather.1
  304.8 102.3 reduce-scatter.1
